TPU v7x, 32 devices: a whole 2x2x4 slice. The times are simulated.
32 devices in a mesh: adapter: 8 (over z, y), tensor: 4 (over x, core).
Axes of the slice: x: 2, y: 2, z: 4, core: 2. Of those that a mesh axis runs over, the one named last changes fastest.
Arguments:
- hidden: bfloat16 [768, 2, 8192], P('adapter'), may hold values from -6 to 6
- input_norm_gain: bfloat16 [8192], replicated, may hold values from 0.25 to 1.75
- key_value_weight: bfloat16 [8192, 2, 1024], P(None, None, 'tensor'), may hold values from -0.0625 to 0.0625
- adapter_down_weight: bfloat16 [32, 8192, 128], P('adapter', 'tensor'), may hold values from -0.0625 to 0.0625
- adapter_up_weight: bfloat16 [32, 2, 64, 1024], P('adapter', None, None, 'tensor'), may hold values from -0.375 to 0.375
- request_adapter: int32 [768], P('adapter'), may hold values from 0 to 31, as said below
- queries: bfloat16 [768, 2, 8192], P('adapter', None, 'tensor'), may hold values from -100 to 100
- cached_key_rows: bfloat16 [768, 64, 1024], P('adapter', None, 'tensor'), may hold values from -5 to 5
- cached_value_rows: bfloat16 [768, 64, 1024], P('adapter', None, 'tensor'), may hold values from -6 to 6
- cached_length: int32 [768], P('adapter'), may hold values from 2 to 64, as said below
Outputs:
- new_keys: bfloat16 [768, 2, 1024], P('adapter', None, 'tensor')
- new_values: bfloat16 [768, 2, 1024], P('adapter', None, 'tensor')
- attended: bfloat16 [768, 2, 8192], P('adapter', None, 'tensor')
Inputs may be any that keep to these rules, and one draw needn't show every extreme that they name: `request_adapter`: adapter a is held by adapter index a // 4. Of the requests on one adapter index at most 24 name adapters held by one adapter index, and in every draw one adapter index is named by exactly 24 requests of every adapter index. `cached_length`: some request has exactly 64 cached tokens.
All inputs are finite; a program needn't handle non-finite values.
Results may differ from a plain program's by a relative error of at most 0.0055.
Values may be sent and summed in bfloat16 or wider, within the bound.
A program may use at most 128 MiB of HBM per device.

v0:
```python
import functools

import jax
import jax.numpy as jnp
from jax import lax
from jax.experimental import pallas as pl
from jax.experimental.pallas import tpu as pltpu
from jax.sharding import PartitionSpec as P

HEAD_DIM = 128


epsilon = 1e-05
rope_base = 500000.0


def rotate_keys(key_vecs, positions):
    head_size = key_vecs.shape[-1]
    half_size = head_size // 2
    inverse = rope_base ** (-(jnp.arange(half_size, dtype=jnp.float32) * 2.0 / head_size))
    angles = positions[..., None] * inverse
    cosine = jnp.cos(angles)
    sine_part = jnp.sin(angles)
    first_half = key_vecs[..., :half_size]
    second = key_vecs[..., half_size:]
    return jnp.concatenate(
        [first_half * cosine - second * sine_part, second * cosine + first_half * sine_part],
        axis=-1,
    )


def normalize(hidden, input_norm_gain):
    values = hidden.astype(jnp.float32)
    meansq = jnp.mean(values * values, axis=-1, keepdims=True)
    return (values * lax.rsqrt(meansq + epsilon) * input_norm_gain.astype(jnp.float32)).astype(
        jnp.bfloat16
    )


MESH = pl.DeviceIdType.MESH


def route(request_adapter, adapter_number, capacity, owner_total, token_count):
    me = lax.axis_index("adapter")
    rows = request_adapter.shape[0]
    relative = jnp.mod(request_adapter // adapter_number - me, owner_total)
    same = relative[:, None] == relative[None, :]
    order = jnp.arange(rows, dtype=jnp.int32)
    earlier = order[None, :] < order[:, None]
    rank = jnp.sum((same & earlier).astype(jnp.int32), axis=1)
    tokens = jnp.arange(token_count, dtype=jnp.int32)
    place = (relative[None, :] * token_count + tokens[:, None]) * capacity + rank[None, :]
    places = jnp.arange(owner_total * token_count * capacity, dtype=jnp.int32)
    return place.reshape(-1)[:, None] == places[None, :]


def exchange(blocks, owner_total):
    received = {0: blocks[0]}
    middle = owner_total // 2
    for step in sorted(range(1, owner_total), key=lambda step: abs(step - middle)):
        pairs = [(source, (source + step) % owner_total) for source in range(owner_total)]
        received[step] = lax.ppermute(blocks[step], "adapter", pairs)
    return jnp.stack([received[step] for step in range(owner_total)])


def return_kernel(
    owners,
    shards,
    adapters,
    partial_ref,
    names_ref,
    up_ref,
    selector_ref,
    base_ref,
    out_ref,
    parts,
    delta,
    returned,
    part_send,
    part_recv,
    back_send,
    back_recv,
):
    me = lax.axis_index("adapter")
    mine = lax.axis_index("tensor")
    barrier = pltpu.get_barrier_semaphore()
    for step in range(1, owners):
        pl.semaphore_signal(
            barrier, inc=1, device_id=(lax.rem(me + step, owners), mine), device_id_type=MESH
        )
    for step in range(1, shards):
        pl.semaphore_signal(
            barrier, inc=1, device_id=(me, lax.rem(mine + step, shards)), device_id_type=MESH
        )
    pl.semaphore_wait(barrier, owners + shards - 2)

    def part_copy(block, step):
        return pltpu.make_async_remote_copy(
            src_ref=partial_ref.at[block],
            dst_ref=parts.at[step - 1, block],
            send_sem=part_send.at[step - 1, block],
            recv_sem=part_recv.at[step - 1, block],
            device_id=(me, lax.rem(mine + step, shards)),
            device_id_type=MESH,
        )

    def back_copy(block):
        return pltpu.make_async_remote_copy(
            src_ref=delta.at[block],
            dst_ref=returned.at[block],
            send_sem=back_send.at[block],
            recv_sem=back_recv.at[block],
            device_id=(lax.rem(me - block + owners, owners), mine),
            device_id_type=MESH,
        )

    def send_parts(block):
        for step in range(1, shards):
            part_copy(block, step).start()

    def adapter_terms(block):
        total = partial_ref[block]
        for step in range(1, shards):
            part_copy(block, step).wait_recv()
            total = total + parts[step - 1, block]
        names = names_ref[block].astype(jnp.float32)
        spread = jnp.concatenate(
            [jnp.where(names == float(a + 1), total, 0.0) for a in range(adapters)], axis=1
        ).astype(jnp.bfloat16)
        terms = jnp.dot(spread, up_ref[...], preferred_element_type=jnp.float32)
        return terms.astype(jnp.bfloat16)

    @pl.loop(1, owners)
    def _(block):
        send_parts(block)

    send_parts(0)

    @pl.loop(1, owners)
    def _(block):
        delta[block] = adapter_terms(block)
        back_copy(block).start()

    returned[0] = adapter_terms(0)

    @pl.loop(1, owners)
    def _(block):
        back_copy(block).wait_recv()

    rows = returned.shape[0] * returned.shape[1]
    out_ref[...] = base_ref[...] + jnp.dot(
        selector_ref[...],
        returned[...].reshape(rows, returned.shape[2]),
        preferred_element_type=jnp.float32,
    )

    @pl.loop(1, owners)
    def _(block):
        back_copy(block).wait_send()

    @pl.loop(0, owners)
    def _(block):
        for step in range(1, shards):
            part_copy(block, step).wait_send()


def return_terms(partial, names, up_matrix, selector, base, adapters):
    owners, rows, width = partial.shape
    shards = lax.axis_size("tensor")
    columns = base.shape[1]
    return pl.pallas_call(
        functools.partial(return_kernel, owners, shards, adapters),
        out_shape=jax.ShapeDtypeStruct(base.shape, jnp.float32),
        in_specs=[pl.BlockSpec(memory_space=pltpu.VMEM)] * 5,
        out_specs=pl.BlockSpec(memory_space=pltpu.VMEM),
        scratch_shapes=[
            pltpu.VMEM((shards - 1, owners, rows, width), jnp.float32),
            pltpu.VMEM((owners, rows, columns), jnp.bfloat16),
            pltpu.VMEM((owners, rows, columns), jnp.bfloat16),
            pltpu.SemaphoreType.DMA((shards - 1, owners)),
            pltpu.SemaphoreType.DMA((shards - 1, owners)),
            pltpu.SemaphoreType.DMA((owners,)),
            pltpu.SemaphoreType.DMA((owners,)),
        ],
        compiler_params=pltpu.CompilerParams(
            collective_id=0, has_side_effects=True, vmem_limit_bytes=24 * 1024 * 1024
        ),
    )(partial, names, up_matrix, selector, base)


def cache_part(queries, cached_key_rows, cached_value_rows, cached_length):
    row_total, token_total, query_width = queries.shape
    context = cached_key_rows.shape[1]
    kv_local = cached_key_rows.shape[2] // HEAD_DIM
    group_size = query_width // (kv_local * HEAD_DIM)
    score_scale = float(HEAD_DIM) ** (-0.5)
    query_vecs = queries.reshape(row_total, token_total, kv_local, group_size, HEAD_DIM)
    cache_vecs = cached_key_rows.reshape(row_total, context, kv_local, HEAD_DIM)
    cache_vals = cached_value_rows.reshape(row_total, context, kv_local, HEAD_DIM)
    scores = (
        jnp.einsum("rthgd,rjhd->rthgj", query_vecs, cache_vecs, preferred_element_type=jnp.float32)
        * score_scale
    )
    slot_live = jnp.arange(context, dtype=jnp.int32)[None, :] < cached_length[:, None]
    scores = jnp.where(slot_live[:, None, None, None, :], scores, -1e30)
    top = jnp.max(scores, axis=-1, keepdims=True)
    weights = jnp.exp(scores - top)
    total = jnp.sum(weights, axis=-1, keepdims=True)
    mixed = jnp.einsum(
        "rthgj,rjhd->rthgd",
        weights.astype(jnp.bfloat16),
        cache_vals,
        preferred_element_type=jnp.float32,
    )
    return query_vecs, top, total, mixed


def finish(query_vecs, top, total, mixed, new_keys, new_values):
    row_total, token_total, kv_local, group_size, head_size = query_vecs.shape
    score_scale = float(head_size) ** (-0.5)
    fresh_keys = new_keys.reshape(row_total, token_total, kv_local, head_size)
    fresh_vals = new_values.reshape(row_total, token_total, kv_local, head_size)
    scores = (
        jnp.einsum("rthgd,rshd->rthgs", query_vecs, fresh_keys, preferred_element_type=jnp.float32)
        * score_scale
    )
    order = jnp.arange(token_total, dtype=jnp.int32)
    causal = order[:, None] >= order[None, :]
    scores = jnp.where(causal[None, :, None, None, :], scores, -1e30)
    peak = jnp.maximum(top, jnp.max(scores, axis=-1, keepdims=True))
    scale = jnp.exp(top - peak)
    weights = jnp.exp(scores - peak)
    denominator = scale * total + jnp.sum(weights, axis=-1, keepdims=True)
    out = mixed * (scale / denominator)
    probs = weights / denominator
    for s in range(token_total):
        out = out + probs[..., s : s + 1] * fresh_vals[:, None, s, :, None, :].astype(jnp.float32)
    return out.reshape(row_total, token_total, -1).astype(jnp.bfloat16)


def body(
    hidden,
    input_norm_gain,
    key_value_weight,
    adapter_down_weight,
    adapter_up_weight,
    request_adapter,
    queries,
    cached_key_rows,
    cached_value_rows,
    cached_length,
):
    row_count, token_count, model_width = hidden.shape
    feature_total = adapter_down_weight.shape[1]
    adapter_number = adapter_down_weight.shape[0]
    column_count = key_value_weight.shape[2]
    owner_total = lax.axis_size("adapter")
    capacity = -(-(2 * row_count // owner_total) // 8) * 8
    block_rows = token_count * capacity
    normed = normalize(jnp.swapaxes(hidden, 0, 1), input_norm_gain)
    normed = normed.reshape(token_count * row_count, model_width)
    feature_start = lax.axis_index("tensor") * feature_total
    own = lax.dynamic_slice_in_dim(normed, feature_start, feature_total, 1)
    selector = route(request_adapter, adapter_number, capacity, owner_total, token_count)
    selector = selector.astype(jnp.bfloat16)
    marks = jnp.tile((request_adapter % adapter_number + 1).astype(jnp.bfloat16), token_count)
    marks = jnp.broadcast_to(marks[:, None], (token_count * row_count, HEAD_DIM))
    packed = jnp.dot(
        selector.T, jnp.concatenate([own, marks], axis=1), preferred_element_type=jnp.float32
    ).astype(jnp.bfloat16)
    received = exchange(packed.reshape(owner_total, block_rows, packed.shape[1]), owner_total)

    base_proj = jnp.concatenate(
        [
            jnp.dot(normed, key_value_weight[:, kind], preferred_element_type=jnp.float32)
            for kind in range(2)
        ],
        axis=1,
    )
    query_vecs, top, total, mixed = cache_part(
        queries, cached_key_rows, cached_value_rows, cached_length
    )
    rank_width = adapter_up_weight.shape[2]
    zero = jnp.zeros((adapter_number, rank_width, column_count), jnp.bfloat16)
    up_matrix = jnp.concatenate(
        [
            jnp.concatenate([adapter_up_weight[:, 0], zero], axis=2),
            jnp.concatenate([zero, adapter_up_weight[:, 1]], axis=2),
        ],
        axis=1,
    ).reshape(adapter_number * 2 * rank_width, 2 * column_count)
    received, base_proj, up_matrix, query_vecs, top, total, mixed = lax.optimization_barrier(
        (received, base_proj, up_matrix, query_vecs, top, total, mixed)
    )

    rows = received[:, :, :feature_total].reshape(owner_total * block_rows, feature_total)
    names = received[:, :, feature_total:]
    owner_name = names[:, :, :1].reshape(owner_total * block_rows, 1).astype(jnp.float32)
    partial = jnp.zeros((owner_total * block_rows, 2 * rank_width), jnp.float32)
    for a in range(adapter_number):
        term = jnp.dot(rows, adapter_down_weight[a], preferred_element_type=jnp.float32)
        partial = partial + jnp.where(owner_name == float(a + 1), term, 0.0)
    partial = partial.reshape(owner_total, block_rows, 2 * rank_width)
    projected = return_terms(partial, names, up_matrix, selector, base_proj, adapter_number)
    projected_output = jnp.swapaxes(
        projected.reshape(token_count, row_count, 2, column_count), 0, 1
    )

    positions = (cached_length[:, None] + jnp.arange(token_count, dtype=jnp.int32)[None, :]).astype(
        jnp.float32
    )
    kv_local = column_count // HEAD_DIM
    key_vecs = rotate_keys(
        projected_output[:, :, 0].reshape(row_count, token_count, kv_local, HEAD_DIM),
        positions[:, :, None],
    )
    new_keys = key_vecs.reshape(row_count, token_count, column_count).astype(jnp.bfloat16)
    new_values = projected_output[:, :, 1].astype(jnp.bfloat16)
    attended = finish(query_vecs, top, total, mixed, new_keys, new_values)
    return (new_keys, new_values, attended)


def solution(mesh):
    in_specs = (
        P("adapter", None, None),
        P(),
        P(None, None, "tensor"),
        P("adapter", "tensor", None),
        P("adapter", None, None, "tensor"),
        P("adapter"),
        P("adapter", None, "tensor"),
        P("adapter", None, "tensor"),
        P("adapter", None, "tensor"),
        P("adapter"),
    )
    out_specs = (
        P("adapter", None, "tensor"),
        P("adapter", None, "tensor"),
        P("adapter", None, "tensor"),
    )
    return jax.shard_map(body, mesh=mesh, in_specs=in_specs, out_specs=out_specs, check_vma=False)
```

profile of v0, /device:TPU:0, one launch (start us, length us, event | category | flops | bytes accessed | tf_op | source)
XLA Modules:
  0.0 115.2 jit_solution(8785921184323791807)
XLA Ops:
  2.3 5.2 %fusion = f32[2,96]{1,0:T(2,128)S(1)} fusion(bf16[96,2,8192]{2,1,0:T(2,128)(2,1)} %param.10), kind=kLoop, calls=%fused_computation.2 | loop fusion | flops 4718400 | bytes 3146496 | tf_op jit(solution)/shard_map/reduce_sum | solution.py:34
  7.8 4.4 %fusion.2 = bf16[2,96,8192]{2,1,0:T(8,128)(2,1)} fusion(f32[8192]{0:T(1024)S(1)} %convert_element_type.100, f32[2,96]{1,0:T(2,128)S(1)} %add_rsqrt_fusion, bf16[96,2,8192]{2,1,0:T(2,128)(2,1)S(1)} %copy-done), kind=kLoop, calls=%fused_computation.4 | loop fusion | flops 6291456 | bytes 6324992 | tf_op jit(solution)/shard_map/convert_element_type | solution.py:35
  12.2 1.2 %constant_dynamic-slice_fusion = bf16[192,2048]{1,0:T(8,128)(2,1)S(1)} fusion(bf16[192,8192]{1,0:T(8,128)(2,1)} %bitcast.145, s32[]{:T(128)S(6)} %select_n.45), kind=kLoop, calls=%fused_computation.117 | loop fusion | bytes 1572868 | tf_op jit(solution)/shard_map/dynamic_slice | solution.py:263
  14.3 1.1 fusion.60
  15.5 3.0 %collective-permute-start = (bf16[48,2176]{1,0:T(8,128)(2,1)}, bf16[48,2176]{1,0:T(8,128)(2,1)}, u32[]{:S(2)}, u32[]{:S(2)}) collective-permute-start(bf16[48,2176]{1,0:T(8,128)(2,1)} %get-tuple-element.37), channel_id=1, source_target_pairs={{0,4},{4,8},{8,12},{12,16},{16,20},{20,24},{24,28},{28,0},{1,5},{5... | collective-permute-start | bytes 626696 | tf_op jit(solution)/shard_map/ppermute | solution.py:62
  18.4 1.6 %collective-permute-start.1 = (bf16[48,2176]{1,0:T(8,128)(2,1)}, bf16[48,2176]{1,0:T(8,128)(2,1)}, u32[]{:S(2)}, u32[]{:S(2)}) collective-permute-start(bf16[48,2176]{1,0:T(8,128)(2,1)} %get-tuple-element.36), channel_id=1, source_target_pairs={{0,8},{4,12},{8,16},{12,20},{16,24},{20,28},{24,0},{28,4},{1,9},{5... | collective-permute-start | bytes 626696 | tf_op jit(solution)/shard_map/ppermute | solution.py:62
  20.0 2.5 %collective-permute-start.2 = (bf16[48,2176]{1,0:T(8,128)(2,1)}, bf16[48,2176]{1,0:T(8,128)(2,1)}, u32[]{:S(2)}, u32[]{:S(2)}) collective-permute-start(bf16[48,2176]{1,0:T(8,128)(2,1)} %get-tuple-element.35), channel_id=1, source_target_pairs={{0,12},{4,16},{8,20},{12,24},{16,28},{20,0},{24,4},{28,8},{1,13},{... | collective-permute-start | bytes 626696 | tf_op jit(solution)/shard_map/ppermute | solution.py:62
  22.6 1.2 %collective-permute-start.3 = (bf16[48,2176]{1,0:T(8,128)(2,1)}, bf16[48,2176]{1,0:T(8,128)(2,1)}, u32[]{:S(2)}, u32[]{:S(2)}) collective-permute-start(bf16[48,2176]{1,0:T(8,128)(2,1)} %get-tuple-element.34), channel_id=1, source_target_pairs={{0,16},{4,20},{8,24},{12,28},{16,0},{20,4},{24,8},{28,12},{1,17},{... | collective-permute-start | bytes 626696 | tf_op jit(solution)/shard_map/ppermute | solution.py:62
  23.8 2.6 %collective-permute-start.4 = (bf16[48,2176]{1,0:T(8,128)(2,1)}, bf16[48,2176]{1,0:T(8,128)(2,1)}, u32[]{:S(2)}, u32[]{:S(2)}) collective-permute-start(bf16[48,2176]{1,0:T(8,128)(2,1)} %get-tuple-element.33), channel_id=1, source_target_pairs={{0,20},{4,24},{8,28},{12,0},{16,4},{20,8},{24,12},{28,16},{1,21},{... | collective-permute-start | bytes 626696 | tf_op jit(solution)/shard_map/ppermute | solution.py:62
  28.0 16.9 %fusion.59 = (bf16[8192,1,256]{2,1,0:T(2,128)(2,1)S(1)}, bf16[8192,1,256]{2,1,0:T(2,128)(2,1)S(1)}) fusion(bf16[8192,2,256]{2,1,0:T(2,128)(2,1)} %param.12), kind=kLoop, calls=%fused_computation.119 | loop fusion | bytes 16777216 | tf_op jit(solution)/shard_map/slice | solution.py:275
  44.8 1.7 %fusion.3 = f32[192,256]{1,0:T(8,128)} fusion(bf16[192,8192]{1,0:T(8,128)(2,1)S(1)} %bitcast.146, bf16[8192,1,256]{2,1,0:T(2,128)(2,1)S(1)} %get-tuple-element.30), kind=kOutput, calls=%fused_computation.7 | convolution fusion | flops 805306368 | bytes 7536640 | tf_op jit(solution)/shard_map/dot_general | solution.py:275
  46.5 1.7 %fusion.4 = f32[192,256]{1,0:T(8,128)} fusion(bf16[192,8192]{1,0:T(8,128)(2,1)S(1)} %bitcast.147, bf16[8192,1,256]{2,1,0:T(2,128)(2,1)S(1)} %get-tuple-element.29), kind=kOutput, calls=%fused_computation.9 | convolution fusion | flops 805306368 | bytes 7536640 | tf_op jit(solution)/shard_map/dot_general | solution.py:275
  48.9 3.1 %reshape.216 = bf16[96,2,2,8,128]{4,3,2,1,0:T(8,128)(2,1)} reshape(bf16[96,2,2048]{2,1,0:T(2,128)(2,1)} %param.16) | data formatting | bytes 1572864 | tf_op jit(solution)/shard_map/reshape | solution.py:197
  52.0 3.0 %reshape.217 = bf16[96,64,2,128]{3,2,1,0:T(2,128)(2,1)} reshape(bf16[96,64,256]{2,1,0:T(8,128)(2,1)S(1)} %copy-done.2) | data formatting | bytes 6291456 | tf_op jit(solution)/shard_map/reshape | solution.py:198
  55.0 3.8 %reshape.218 = bf16[96,64,2,128]{3,2,1,0:T(2,128)(2,1)S(1)} reshape(bf16[96,64,256]{2,1,0:T(8,128)(2,1)} %param.18) | data formatting | bytes 6291456 | tf_op jit(solution)/shard_map/reshape | solution.py:199
  58.8 4.0 %bitcast_reduce_fusion = (f32[96,2,2,8]{3,1,2,0:T(2,128)S(1)}, f32[96,2,64,2,8]{2,4,3,1,0:T(8,128)S(1)}) fusion(bf16[96,2,2,8,128]{4,3,2,1,0:T(8,128)(2,1)} %reshape.216, bf16[96,64,2,128,1]{3,2,1,0,4:T(2,128)(2,1)} %bitcast.149, pred[96,64]{1,0:T(8,128)(4,1)S(1)} %iota_compare_fusion.4), kind=kOutput, calls=%fused_computation.15 | convolution fusion | flops 50918400 | bytes 4737024 | tf_op jit(solution)/shard_map/rthgd,rjhd->rthgj/dot_general | solution.py:201
  62.8 1.1 fusion.16
  64.0 2.2 %fusion.12 = f32[96,2,2,8,128]{4,3,1,2,0:T(8,128)} fusion(bf16[96,64,2,128,1]{3,2,1,0,4:T(2,128)(2,1)S(1)} %bitcast.148, f32[96,2,64,2,8]{2,4,3,1,0:T(8,128)S(1)} %get-tuple-element.52, f32[96,2,2,8]{3,1,2,0:T(2,128)S(1)} %get-tuple-element.51), kind=kOutput, calls=%fused_computation.19 | convolution fusion | flops 50724864 | bytes 5517312 | tf_op jit(solution)/shard_map/rthgj,rjhd->rthgd/dot_general | solution.py:209
  66.3 2.3 %multiply_cosine_fusion = (f32[96,2,64]{2,1,0:T(2,128)}, f32[96,2,64]{2,1,0:T(2,128)}) fusion(f32[64]{0:T(128)S(1)} %negate_power_fusion, f32[96,2]{1,0:T(8,128)S(1)} %copy-done.16), kind=kLoop, calls=%fused_computation.89 | loop fusion | flops 12288 | bytes 99328 | tf_op jit(solution)/shard_map/cos | solution.py:22
  68.7 1.4 %collective-permute-start.5 = (bf16[48,2176]{1,0:T(8,128)(2,1)S(1)}, bf16[48,2176]{1,0:T(8,128)(2,1)S(1)}, u32[]{:S(2)}, u32[]{:S(2)}) collective-permute-start(bf16[48,2176]{1,0:T(8,128)(2,1)S(1)} %copy-done.13), channel_id=1, source_target_pairs={{0,24},{4,28},{8,0},{12,4},{16,8},{20,12},{24,16},{28,20},{1,25},{... | collective-permute-start | bytes 626696 | tf_op jit(solution)/shard_map/ppermute | solution.py:62
  70.1 1.0 bitcast_dynamic-update-slice_fusion.6
  71.1 1.7 %collective-permute-start.6 = (bf16[48,2176]{1,0:T(8,128)(2,1)S(1)}, bf16[48,2176]{1,0:T(8,128)(2,1)S(1)}, u32[]{:S(2)}, u32[]{:S(2)}) collective-permute-start(bf16[48,2176]{1,0:T(8,128)(2,1)S(1)} %copy-done.12), channel_id=1, source_target_pairs={{0,28},{4,0},{8,4},{12,8},{16,12},{20,16},{24,20},{28,24},{1,29},{... | collective-permute-start | bytes 626696 | tf_op jit(solution)/shard_map/ppermute | solution.py:62
  72.8 1.0 bitcast_dynamic-update-slice_fusion.5
  73.8 1.0 bitcast_dynamic-update-slice_fusion.4
  74.7 1.0 bitcast_dynamic-update-slice_fusion.3
  75.7 1.0 bitcast_dynamic-update-slice_fusion.2
  76.7 1.1 collective-permute-done.6
  79.0 1.8 %convolution_select_fusion.3 = f32[384,128]{1,0:T(8,128)S(1)} fusion(bf16[384,2048]{1,0:T(8,128)(2,1)S(1)} %bitcast.141, bf16[4,2048,128]{2,1,0:T(8,128)(2,1)} %param.13, pred[384]{0:T(512)(128)(4,1)S(1)} %eq.93), kind=kOutput, calls=%fused_computation.31 | convolution fusion | flops 201375744 | bytes 2294144 | tf_op jit(solution)/shard_map/dot_general | solution.py:301
  82.5 21.0 %shard_map.121 = f32[192,512]{1,0:T(8,128)S(1)} custom-call(f32[8,48,128]{2,1,0:T(8,128)S(1)} %bitcast.140, bf16[8,48,128]{2,1,0:T(8,128)(2,1)S(1)} %slice.111.names_ref, bf16[512,512]{1,0:T(8,128)(2,1)S(1)} %bitcast.139, bf16[192,384]{1,0:T(8,128)(2,1)S(1)} %fusion.40.selector_ref, f32[192,512]{1,0:T(8,128)S(1)} %pad_maximum_fusion.base_ref), custom_call_target="tpu_custom_call" | custom-call | tf_op jit(solution)/shard_map/pallas_call | solution.py:171
  106.4 3.7 %fusion.62 = (f32[96,2,2,8]{3,1,2,0:T(2,128)S(1)}, f32[96,2,2,8,2]{3,4,1,2,0:T(2,128)S(1)}) fusion(bf16[96,2,2,8,128]{4,3,2,1,0:T(8,128)(2,1)S(1)} %copy-done.6, pred[2,2]{1,0:T(4,128)(4,1)S(1)} %iota_compare_fusion.6, bf16[96,2,2,64]{3,1,2,0:T(2,128)(2,1)S(1)} %get-tuple-element.43, bf16[96,2,2,64]{3,1,2,0:T(2,128)(2,1)S(1)} %get-tuple-element.42), kind=kOutput, calls=%fused_computation.122 | convolution fusion | flops 1784832 | bytes 921604 | tf_op jit(solution)/shard_map/rthgd,rshd->rthgs/dot_general | solution.py:224
  112.4 1.5 %add_convert_fusion = bf16[96,2,2,8,128]{4,3,1,2,0:T(8,128)(2,1)S(1)} fusion(f32[96,2,2,8,128]{4,3,1,2,0:T(8,128)S(1)} %copy-done.4, f32[96,2,128]{2,1,0:T(2,128)S(1)} %get-tuple-element.47, f32[96,2,2,8]{3,1,2,0:T(2,128)S(1)} %bitcast.156, f32[96,2,128]{2,1,0:T(2,128)S(1)} %get-tuple-element.46, f32[96,2,2,8]{3,1,2,0:T(2,128)S(1)} %bitcast.155, ...), kind=kLoop, calls=%fused_computation.17 | loop fusion | flops 2359296 | bytes 2592768 | tf_op jit(solution)/shard_map/convert_element_type | solution.py:238
  114.1 1.1 reshape.227
  (88 shorter events, 13.4 us)
Async XLA Ops:
  0.6 7.2 %copy-start = (bf16[96,2,8192]{2,1,0:T(2,128)(2,1)S(1)}, bf16[96,2,8192]{2,1,0:T(2,128)(2,1)}, u32[]{:S(2)}) copy-start(bf16[96,2,8192]{2,1,0:T(2,128)(2,1)} %param.10) | copy-start | bytes 9437188
  14.3 12.8 %copy-start.17 = (s32[96]{0:T(128)S(1)}, s32[96]{0:T(128)}, u32[]{:S(2)}) copy-start(s32[96]{0:T(128)} %param.19) | copy-start | bytes 1156
  15.5 53.2 %collective-permute-start = (bf16[48,2176]{1,0:T(8,128)(2,1)}, bf16[48,2176]{1,0:T(8,128)(2,1)}, u32[]{:S(2)}, u32[]{:S(2)}) collective-permute-start(bf16[48,2176]{1,0:T(8,128)(2,1)} %get-tuple-element.37), channel_id=1, source_target_pairs={{0,4},{4,8},{8,12},{12,16},{16,20},{20,24},{24,28},{28,0},{1,5},{5... | collective-permute-start | bytes 626696 | tf_op jit(solution)/shard_map/ppermute | solution.py:62
  18.4 52.6 %collective-permute-start.1 = (bf16[48,2176]{1,0:T(8,128)(2,1)}, bf16[48,2176]{1,0:T(8,128)(2,1)}, u32[]{:S(2)}, u32[]{:S(2)}) collective-permute-start(bf16[48,2176]{1,0:T(8,128)(2,1)} %get-tuple-element.36), channel_id=1, source_target_pairs={{0,8},{4,12},{8,16},{12,20},{16,24},{20,28},{24,0},{28,4},{1,9},{5... | collective-permute-start | bytes 626696 | tf_op jit(solution)/shard_map/ppermute | solution.py:62
  20.0 53.7 %collective-permute-start.2 = (bf16[48,2176]{1,0:T(8,128)(2,1)}, bf16[48,2176]{1,0:T(8,128)(2,1)}, u32[]{:S(2)}, u32[]{:S(2)}) collective-permute-start(bf16[48,2176]{1,0:T(8,128)(2,1)} %get-tuple-element.35), channel_id=1, source_target_pairs={{0,12},{4,16},{8,20},{12,24},{16,28},{20,0},{24,4},{28,8},{1,13},{... | collective-permute-start | bytes 626696 | tf_op jit(solution)/shard_map/ppermute | solution.py:62
  22.6 52.1 %collective-permute-start.3 = (bf16[48,2176]{1,0:T(8,128)(2,1)}, bf16[48,2176]{1,0:T(8,128)(2,1)}, u32[]{:S(2)}, u32[]{:S(2)}) collective-permute-start(bf16[48,2176]{1,0:T(8,128)(2,1)} %get-tuple-element.34), channel_id=1, source_target_pairs={{0,16},{4,20},{8,24},{12,28},{16,0},{20,4},{24,8},{28,12},{1,17},{... | collective-permute-start | bytes 626696 | tf_op jit(solution)/shard_map/ppermute | solution.py:62
  23.8 51.9 %collective-permute-start.4 = (bf16[48,2176]{1,0:T(8,128)(2,1)}, bf16[48,2176]{1,0:T(8,128)(2,1)}, u32[]{:S(2)}, u32[]{:S(2)}) collective-permute-start(bf16[48,2176]{1,0:T(8,128)(2,1)} %get-tuple-element.33), channel_id=1, source_target_pairs={{0,20},{4,24},{8,28},{12,0},{16,4},{20,8},{24,12},{28,16},{1,21},{... | collective-permute-start | bytes 626696 | tf_op jit(solution)/shard_map/ppermute | solution.py:62
  28.0 16.9 %copy-start.1 = (bf16[2,96,8192]{2,1,0:T(8,128)(2,1)S(1)}, bf16[2,96,8192]{2,1,0:T(8,128)(2,1)}, u32[]{:S(2)}) copy-start(bf16[2,96,8192]{2,1,0:T(8,128)(2,1)} %fusion.2) | copy-start | bytes 9437188
  46.5 1.7 %copy-start.11 = (bf16[4,2,64,256]{3,2,1,0:T(8,128)(2,1)S(1)}, bf16[4,2,64,256]{3,2,1,0:T(8,128)(2,1)}, u32[]{:S(2)}) copy-start(bf16[4,2,64,256]{3,2,1,0:T(8,128)(2,1)} %param.14) | copy-start | bytes 786436
  46.5 5.5 %copy-start.2 = (bf16[96,64,256]{2,1,0:T(8,128)(2,1)S(1)}, bf16[96,64,256]{2,1,0:T(8,128)(2,1)}, u32[]{:S(2)}) copy-start(bf16[96,64,256]{2,1,0:T(8,128)(2,1)} %param.17) | copy-start | bytes 9437188
  63.9 2.2 %copy-start.14 = (f32[192,256]{1,0:T(8,128)S(1)}, f32[192,256]{1,0:T(8,128)}, u32[]{:S(2)}) copy-start(f32[192,256]{1,0:T(8,128)} %fusion.3) | copy-start | bytes 589828
  63.9 2.2 %copy-start.15 = (f32[192,256]{1,0:T(8,128)S(1)}, f32[192,256]{1,0:T(8,128)}, u32[]{:S(2)}) copy-start(f32[192,256]{1,0:T(8,128)} %fusion.4) | copy-start | bytes 589828
  64.0 2.3 %copy-start.7 = (bf16[4,64,256]{2,1,0:T(8,128)(2,1)S(1)}, bf16[4,64,256]{2,1,0:T(8,128)(2,1)}, u32[]{:S(2)}) copy-start(bf16[4,64,256]{2,1,0:T(8,128)(2,1)} %get-tuple-element.44) | copy-start | bytes 393220
  64.0 2.3 %copy-start.8 = (bf16[4,64,256]{2,1,0:T(8,128)(2,1)S(1)}, bf16[4,64,256]{2,1,0:T(8,128)(2,1)}, u32[]{:S(2)}) copy-start(bf16[4,64,256]{2,1,0:T(8,128)(2,1)} %get-tuple-element.45) | copy-start | bytes 393220
  64.0 2.3 %copy-start.16 = (f32[96,2]{1,0:T(8,128)S(1)}, f32[96,2]{1,0:T(8,128)}, u32[]{:S(2)}) copy-start(f32[96,2]{1,0:T(8,128)} %add_convert_fusion.1) | copy-start | bytes 2308
  64.0 4.7 %copy-start.13 = (bf16[48,2176]{1,0:T(8,128)(2,1)S(1)}, bf16[48,2176]{1,0:T(8,128)(2,1)}, u32[]{:S(2)}) copy-start(bf16[48,2176]{1,0:T(8,128)(2,1)} %get-tuple-element.32) | copy-start | bytes 626692
  66.2 4.0 %copy-start.3 = (bf16[8,48,2176]{2,1,0:T(8,128)(2,1)S(1)}, bf16[8,48,2176]{2,1,0:T(8,128)(2,1)}, u32[]{:S(2)}) copy-start(bf16[8,48,2176]{2,1,0:T(8,128)(2,1)} %fusion.41) | copy-start | bytes 5013508
  66.2 4.9 %copy-start.12 = (bf16[48,2176]{1,0:T(8,128)(2,1)S(1)}, bf16[48,2176]{1,0:T(8,128)(2,1)}, u32[]{:S(2)}) copy-start(bf16[48,2176]{1,0:T(8,128)(2,1)} %get-tuple-element.31) | copy-start | bytes 626692
  68.7 7.9 %collective-permute-start.5 = (bf16[48,2176]{1,0:T(8,128)(2,1)S(1)}, bf16[48,2176]{1,0:T(8,128)(2,1)S(1)}, u32[]{:S(2)}, u32[]{:S(2)}) collective-permute-start(bf16[48,2176]{1,0:T(8,128)(2,1)S(1)} %copy-done.13), channel_id=1, source_target_pairs={{0,24},{4,28},{8,0},{12,4},{16,8},{20,12},{24,16},{28,20},{1,25},{... | collective-permute-start | bytes 626696 | tf_op jit(solution)/shard_map/ppermute | solution.py:62
  71.1 6.7 %collective-permute-start.6 = (bf16[48,2176]{1,0:T(8,128)(2,1)S(1)}, bf16[48,2176]{1,0:T(8,128)(2,1)S(1)}, u32[]{:S(2)}, u32[]{:S(2)}) collective-permute-start(bf16[48,2176]{1,0:T(8,128)(2,1)S(1)} %copy-done.12), channel_id=1, source_target_pairs={{0,28},{4,0},{8,4},{12,8},{16,12},{20,16},{24,20},{28,24},{1,29},{... | collective-permute-start | bytes 626696 | tf_op jit(solution)/shard_map/ppermute | solution.py:62
  79.0 1.8 %copy-start.5 = (bf16[4,2048,128]{2,1,0:T(8,128)(2,1)S(1)}, bf16[4,2048,128]{2,1,0:T(8,128)(2,1)}, u32[]{:S(2)}) copy-start(bf16[4,2048,128]{2,1,0:T(8,128)(2,1)} %param.13) | copy-start | bytes 6291460
  103.6 1.6 %copy-start.9 = (f32[96,2,64]{2,1,0:T(2,128)S(1)}, f32[96,2,64]{2,1,0:T(2,128)}, u32[]{:S(2)}) copy-start(f32[96,2,64]{2,1,0:T(2,128)} %get-tuple-element.48) | copy-start | bytes 147460
  103.6 1.6 %copy-start.10 = (f32[96,2,64]{2,1,0:T(2,128)S(1)}, f32[96,2,64]{2,1,0:T(2,128)}, u32[]{:S(2)}) copy-start(f32[96,2,64]{2,1,0:T(2,128)} %get-tuple-element.49) | copy-start | bytes 147460
  103.8 2.6 %copy-start.6 = (bf16[96,2,2,8,128]{4,3,2,1,0:T(8,128)(2,1)S(1)}, bf16[96,2,2,8,128]{4,3,2,1,0:T(8,128)(2,1)}, u32[]{:S(2)}) copy-start(bf16[96,2,2,8,128]{4,3,2,1,0:T(8,128)(2,1)} %reshape.216) | copy-start | bytes 2359300
  111.0 1.4 %copy-start.4 = (f32[96,2,2,8,128]{4,3,1,2,0:T(8,128)S(1)}, f32[96,2,2,8,128]{4,3,1,2,0:T(8,128)}, u32[]{:S(2)}) copy-start(f32[96,2,2,8,128]{4,3,1,2,0:T(8,128)} %fusion.12) | copy-start | bytes 4718596
where the time goes:
time: 116 us; the launch traced here: 115 us
  local copies, waits for them, and re-layouts  39.4 us (34%)
  other arithmetic  21 us (18%)
  Pallas kernels  21 us (18%)
  matrix products  17.5 us (15%)
  starting transfers between devices  14 us (12%)
    pallas_call x1, Pallas kernels, return_terms(): pl.pallas_call(functools.partial(return_kernel, owners, shards, adapters)...  21 us
    slice x1, local copies, waits for them, and re-layouts, body(): key_value_weight[:, kind]  16.9 us
    ppermute x7, starting transfers between devices, exchange(): received[step] = lax.ppermute(blocks[step], 'adapter', pairs)  14 us
    unnamed x45, local copies, waits for them, and re-layouts  7.05 us
    reduce_sum x1, other arithmetic, normalize(): meansq = jnp.mean(values * values, axis=-1, keepdims=True)  5.22 us
    convert_element_type x1, other arithmetic, normalize(): (values * lax.rsqrt(meansq + epsilon) * input_norm_gain.astype(jnp.float3...  4.42 us
    dot_general x1, matrix products, cache_part(): jnp.einsum('rthgd,rjhd->rthgj', query_vecs, cache_vecs, preferred_element...  4.02 us
    reshape x1, local copies, waits for them, and re-layouts, cache_part(): cached_value_rows.reshape(row_total, context, kv_local, HEAD_DIM)  3.75 us
  transfers between devices with their start and end apart: 7, of which 1 were waited for; matrix products, arithmetic and copies ran while one was open for 41% of the time, Pallas kernels for 0%

commit v1 on v0

--- a/solution.py
+++ b/solution.py
@@ -54,33 +54,25 @@
     return place.reshape(-1)[:, None] == places[None, :]
 
 
-def exchange(blocks, owner_total):
-    received = {0: blocks[0]}
-    middle = owner_total // 2
-    for step in sorted(range(1, owner_total), key=lambda step: abs(step - middle)):
+def send_blocks(blocks, steps, owner_total):
+    received = {}
+    for step in steps:
         pairs = [(source, (source + step) % owner_total) for source in range(owner_total)]
         received[step] = lax.ppermute(blocks[step], "adapter", pairs)
-    return jnp.stack([received[step] for step in range(owner_total)])
+    return received
 
 
 def return_kernel(
     owners,
     shards,
     adapters,
-    partial_ref,
-    names_ref,
-    up_ref,
-    selector_ref,
-    base_ref,
-    out_ref,
-    parts,
-    delta,
-    returned,
-    part_send,
-    part_recv,
-    back_send,
-    back_recv,
+    *refs,
 ):
+    blocks = refs[:owners]
+    down_ref, up_ref, selector_ref, base_ref, out_ref, partial_ref, names_ref = refs[
+        owners : owners + 7
+    ]
+    parts, delta, returned, part_send, part_recv, back_send, back_recv = refs[owners + 7 :]
     me = lax.axis_index("adapter")
     mine = lax.axis_index("tensor")
     barrier = pltpu.get_barrier_semaphore()
@@ -130,11 +122,18 @@
         terms = jnp.dot(spread, up_ref[...], preferred_element_type=jnp.float32)
         return terms.astype(jnp.bfloat16)
 
-    @pl.loop(1, owners)
-    def _(block):
+    features = down_ref.shape[1]
+    for block in [*range(1, owners), 0]:
+        names = blocks[block][:, features:]
+        names_ref[block] = names
+        names = names.astype(jnp.float32)
+        rows = blocks[block][:, :features]
+        total = jnp.zeros(names.shape, jnp.float32)
+        for a in range(adapters):
+            term = jnp.dot(rows, down_ref[a], preferred_element_type=jnp.float32)
+            total = total + jnp.where(names == float(a + 1), term, 0.0)
+        partial_ref[block] = total
         send_parts(block)
-
-    send_parts(0)
 
     @pl.loop(1, owners)
     def _(block):
@@ -164,16 +163,20 @@
             part_copy(block, step).wait_send()
 
 
-def return_terms(partial, names, up_matrix, selector, base, adapters):
-    owners, rows, width = partial.shape
+def return_terms(blocks, down_weight, up_matrix, selector, base):
+    owners = len(blocks)
+    rows = blocks[0].shape[0]
+    adapters, _, width = down_weight.shape
     shards = lax.axis_size("tensor")
     columns = base.shape[1]
     return pl.pallas_call(
         functools.partial(return_kernel, owners, shards, adapters),
         out_shape=jax.ShapeDtypeStruct(base.shape, jnp.float32),
-        in_specs=[pl.BlockSpec(memory_space=pltpu.VMEM)] * 5,
+        in_specs=[pl.BlockSpec(memory_space=pltpu.VMEM)] * (owners + 4),
         out_specs=pl.BlockSpec(memory_space=pltpu.VMEM),
         scratch_shapes=[
+            pltpu.VMEM((owners, rows, width), jnp.float32),
+            pltpu.VMEM((owners, rows, width), jnp.bfloat16),
             pltpu.VMEM((shards - 1, owners, rows, width), jnp.float32),
             pltpu.VMEM((owners, rows, columns), jnp.bfloat16),
             pltpu.VMEM((owners, rows, columns), jnp.bfloat16),
@@ -185,7 +188,7 @@
         compiler_params=pltpu.CompilerParams(
             collective_id=0, has_side_effects=True, vmem_limit_bytes=24 * 1024 * 1024
         ),
-    )(partial, names, up_matrix, selector, base)
+    )(*blocks, down_weight, up_matrix, selector, base)
 
 
 def cache_part(queries, cached_key_rows, cached_value_rows, cached_length):
@@ -268,7 +271,12 @@
     packed = jnp.dot(
         selector.T, jnp.concatenate([own, marks], axis=1), preferred_element_type=jnp.float32
     ).astype(jnp.bfloat16)
-    received = exchange(packed.reshape(owner_total, block_rows, packed.shape[1]), owner_total)
+    blocks = packed.reshape(owner_total, block_rows, packed.shape[1])
+    blocks = [blocks[step] for step in range(owner_total)]
+    middle = owner_total // 2
+    steps = sorted(range(1, owner_total), key=lambda step: abs(step - middle))
+    early, late = steps[:5], steps[5:]
+    received = send_blocks(blocks, early, owner_total)
 
     base_proj = jnp.concatenate(
         [
@@ -277,6 +285,13 @@
         ],
         axis=1,
     )
+    waiting = {step: blocks[step] for step in late}
+    arrived = {step: received[step] for step in early[:2]}
+    waiting, arrived, base_proj, queries = lax.optimization_barrier(
+        (waiting, arrived, base_proj, queries)
+    )
+    received.update(arrived)
+    received.update(send_blocks(waiting, late, owner_total))
     query_vecs, top, total, mixed = cache_part(
         queries, cached_key_rows, cached_value_rows, cached_length
     )
@@ -293,15 +308,14 @@
         (received, base_proj, up_matrix, query_vecs, top, total, mixed)
     )
 
-    rows = received[:, :, :feature_total].reshape(owner_total * block_rows, feature_total)
-    names = received[:, :, feature_total:]
-    owner_name = names[:, :, :1].reshape(owner_total * block_rows, 1).astype(jnp.float32)
-    partial = jnp.zeros((owner_total * block_rows, 2 * rank_width), jnp.float32)
-    for a in range(adapter_number):
-        term = jnp.dot(rows, adapter_down_weight[a], preferred_element_type=jnp.float32)
-        partial = partial + jnp.where(owner_name == float(a + 1), term, 0.0)
-    partial = partial.reshape(owner_total, block_rows, 2 * rank_width)
-    projected = return_terms(partial, names, up_matrix, selector, base_proj, adapter_number)
+    received[0] = blocks[0]
+    projected = return_terms(
+        [received[step] for step in range(owner_total)],
+        adapter_down_weight,
+        up_matrix,
+        selector,
+        base_proj,
+    )
     projected_output = jnp.swapaxes(
         projected.reshape(token_count, row_count, 2, column_count), 0, 1
     )

time: 116 us -> 106 us (0.914)
  local copies, waits for them, and re-layouts: 39.4 us -> 32.3 us
  other arithmetic: 21 us -> 19.2 us
  starting transfers between devices: 14 us -> 15.6 us
  Pallas kernels: 21 us -> 19.8 us
    unnamed x45 -> x28, local copies, waits for them, and re-layouts: 7.05 us -> 2.87 us
    slice x1, local copies, waits for them, and re-layouts: 16.9 us -> 12.9 us  [body(): key_value_weight[:, kind]]
    dot_general x4 -> x0, matrix products: 3.49 us -> none  [body(): jnp.dot(rows, adapter_down_weight[a], preferred_element_type=jnp.float32)]
    dot_general x2, matrix products: 3.32 us -> 6.67 us  [body(): jnp.dot(normed, key_value_weight[:, kind], preferred_element_type=jnp.flo...]
    reshape x1, local copies, waits for them, and re-layouts: 3 us -> 5.49 us  [cache_part(): cache_vecs = cached_key_rows.reshape(row_total, context, kv_local, HEAD_DIM)]
    reshape x1, local copies, waits for them, and re-layouts: 3.75 us -> 5.58 us  [cache_part(): cached_value_rows.reshape(row_total, context, kv_local, HEAD_DIM)]
    convert_element_type x1, other arithmetic: 4.42 us -> 2.88 us  [normalize(): (values * lax.rsqrt(meansq + epsilon) * input_norm_gain.astype(jnp.float3...]
    ppermute x7, starting transfers between devices: 14 us -> 15.6 us  [send_blocks(): received[step] = lax.ppermute(blocks[step], 'adapter', pairs)]
  transfers between devices with their start and end apart: 7 -> 7, of which waited for: 1 -> 0; matrix products, arithmetic and copies ran while one was open for 41% -> 41% of each run, Pallas kernels for 0% -> 0%
where the time goes in v1:
time: 106 us; the launch traced here: 105 us
  local copies, waits for them, and re-layouts  32.3 us (30%)
  Pallas kernels  19.8 us (19%)
  other arithmetic  19.2 us (18%)
  matrix products  17.1 us (16%)
  starting transfers between devices  15.6 us (15%)
  between operations  1.06 us (1%)
    pallas_call x1, Pallas kernels, return_terms(): pl.pallas_call(functools.partial(return_kernel, owners, shards, adapters)...  19.8 us
    ppermute x7, starting transfers between devices, send_blocks(): received[step] = lax.ppermute(blocks[step], 'adapter', pairs)  15.6 us
    slice x1, local copies, waits for them, and re-layouts, body(): key_value_weight[:, kind]  12.9 us
    dot_general x2, matrix products, body(): jnp.dot(normed, key_value_weight[:, kind], preferred_element_type=jnp.flo...  6.67 us
    reshape x1, local copies, waits for them, and re-layouts, cache_part(): cached_value_rows.reshape(row_total, context, kv_local, HEAD_DIM)  5.58 us
    reshape x1, local copies, waits for them, and re-layouts, cache_part(): cache_vecs = cached_key_rows.reshape(row_total, context, kv_local, HEAD_DIM)  5.49 us
    reduce_sum x1, other arithmetic, normalize(): meansq = jnp.mean(values * values, axis=-1, keepdims=True)  5.3 us
    dot_general x1, matrix products, cache_part(): jnp.einsum('rthgd,rjhd->rthgj', query_vecs, cache_vecs, preferred_element...  3.82 us
  transfers between devices with their start and end apart: 7, of which 0 were waited for; matrix products, arithmetic and copies ran while one was open for 41% of the time, Pallas kernels for 0%

profile of v1, /device:TPU:0, one launch (start us, length us, event | category | flops | bytes accessed | tf_op | source)
XLA Modules:
  0.0 105.1 jit_solution(1037366900965600385)
XLA Ops:
  0.7 0.9 convert_element_type.82
  1.5 5.3 %fusion = f32[2,96]{1,0:T(2,128)S(1)} fusion(bf16[96,2,8192]{2,1,0:T(2,128)(2,1)} %param.10), kind=kLoop, calls=%fused_computation.2 | loop fusion | flops 4718400 | bytes 3146496 | tf_op jit(solution)/shard_map/reduce_sum | solution.py:34
  7.2 2.9 %fusion.2 = bf16[2,96,8192]{2,1,0:T(8,128)(2,1)S(1)} fusion(f32[8192]{0:T(1024)S(1)} %convert_element_type.82, f32[2,96]{1,0:T(2,128)S(1)} %add_rsqrt_fusion, bf16[96,2,8192]{2,1,0:T(2,128)(2,1)S(1)} %copy-done.2), kind=kLoop, calls=%fused_computation.4 | loop fusion | flops 6291456 | bytes 6324992 | tf_op jit(solution)/shard_map/convert_element_type | solution.py:35
  10.2 1.6 %copy-done.3 = bf16[2,96,8192]{2,1,0:T(8,128)(2,1)} copy-done((bf16[2,96,8192]{2,1,0:T(8,128)(2,1)}, bf16[2,96,8192]{2,1,0:T(8,128)(2,1)S(1)}, u32[]{:S(2)}) %copy-start.3) | copy-done | bytes 3145752
  11.9 0.8 convolution_convert_fusion
  12.7 0.9 fusion.44
  13.6 4.0 %collective-permute-start = (bf16[48,2176]{1,0:T(8,128)(2,1)}, bf16[48,2176]{1,0:T(8,128)(2,1)S(1)}, u32[]{:S(2)}, u32[]{:S(2)}) collective-permute-start(bf16[48,2176]{1,0:T(8,128)(2,1)} %get-tuple-element.55), channel_id=1, source_target_pairs={{0,12},{4,16},{8,20},{12,24},{16,28},{20,0},{24,4},{28,8},{1,13},{... | collective-permute-start | bytes 626696 | tf_op jit(solution)/shard_map/ppermute | solution.py:61
  17.6 2.6 %collective-permute-start.1 = (bf16[48,2176]{1,0:T(8,128)(2,1)S(1)}, bf16[48,2176]{1,0:T(8,128)(2,1)S(1)}, u32[]{:S(2)}, u32[]{:S(2)}) collective-permute-start(bf16[48,2176]{1,0:T(8,128)(2,1)S(1)} %get-tuple-element.54), channel_id=1, source_target_pairs={{0,16},{4,20},{8,24},{12,28},{16,0},{20,4},{24,8},{28,12},{1,17},{... | collective-permute-start | bytes 626696 | tf_op jit(solution)/shard_map/ppermute | solution.py:61
  20.4 2.6 %collective-permute-start.4 = (bf16[48,2176]{1,0:T(8,128)(2,1)}, bf16[48,2176]{1,0:T(8,128)(2,1)S(1)}, u32[]{:S(2)}, u32[]{:S(2)}) collective-permute-start(bf16[48,2176]{1,0:T(8,128)(2,1)} %get-tuple-element.52), channel_id=1, source_target_pairs={{0,20},{4,24},{8,28},{12,0},{16,4},{20,8},{24,12},{28,16},{1,21},{... | collective-permute-start | bytes 626696 | tf_op jit(solution)/shard_map/ppermute | solution.py:61
  23.1 1.3 %collective-permute-start.5 = (bf16[48,2176]{1,0:T(8,128)(2,1)}, bf16[48,2176]{1,0:T(8,128)(2,1)S(1)}, u32[]{:S(2)}, u32[]{:S(2)}) collective-permute-start(bf16[48,2176]{1,0:T(8,128)(2,1)} %get-tuple-element.51), channel_id=1, source_target_pairs={{0,24},{4,28},{8,0},{12,4},{16,8},{20,12},{24,16},{28,20},{1,25},{... | collective-permute-start | bytes 626696 | tf_op jit(solution)/shard_map/ppermute | solution.py:61
  24.6 12.9 %fusion.43 = (bf16[8192,1,256]{2,1,0:T(2,128)(2,1)S(1)}, bf16[8192,1,256]{2,1,0:T(2,128)(2,1)}) fusion(bf16[8192,2,256]{2,1,0:T(2,128)(2,1)S(1)} %copy-done.1), kind=kLoop, calls=%fused_computation.87 | loop fusion | bytes 16777216 | tf_op jit(solution)/shard_map/slice | solution.py:283
  37.5 5.5 %fusion.3 = f32[192,256]{1,0:T(8,128)S(1)} fusion(bf16[192,8192]{1,0:T(8,128)(2,1)} %bitcast.106, bf16[8192,1,256]{2,1,0:T(2,128)(2,1)} %get-tuple-element.50), kind=kOutput, calls=%fused_computation.7 | convolution fusion | flops 805306368 | bytes 7536640 | tf_op jit(solution)/shard_map/dot_general | solution.py:283
  42.9 1.2 %fusion.4 = f32[192,256]{1,0:T(8,128)S(1)} fusion(bf16[192,8192]{1,0:T(8,128)(2,1)S(1)} %bitcast.107, bf16[8192,1,256]{2,1,0:T(2,128)(2,1)S(1)} %get-tuple-element.49), kind=kOutput, calls=%fused_computation.9 | convolution fusion | flops 805306368 | bytes 7536640 | tf_op jit(solution)/shard_map/dot_general | solution.py:283
  44.2 5.5 %reshape.178 = bf16[96,64,2,128]{3,2,1,0:T(2,128)(2,1)} reshape(bf16[96,64,256]{2,1,0:T(8,128)(2,1)} %param.17) | data formatting | bytes 6291456 | tf_op jit(solution)/shard_map/reshape | solution.py:201
  49.7 5.6 %reshape.179 = bf16[96,64,2,128]{3,2,1,0:T(2,128)(2,1)} reshape(bf16[96,64,256]{2,1,0:T(8,128)(2,1)} %param.18) | data formatting | bytes 6291456 | tf_op jit(solution)/shard_map/reshape | solution.py:202
  55.4 2.3 %multiply_cosine_fusion = (f32[96,2,64]{2,1,0:T(2,128)}, f32[96,2,64]{2,1,0:T(2,128)}) fusion(f32[64]{0:T(128)S(1)} %negate_power_fusion, f32[96,2]{1,0:T(8,128)S(1)} %add_convert_fusion.1), kind=kLoop, calls=%fused_computation.57 | loop fusion | flops 12288 | bytes 99328 | tf_op jit(solution)/shard_map/cos | solution.py:22
  57.9 2.4 %reshape.177 = bf16[96,2,2,8,128]{4,3,2,1,0:T(8,128)(2,1)S(1)} reshape(bf16[96,2,2048]{2,1,0:T(2,128)(2,1)} %param.16) | data formatting | bytes 1572864 | tf_op jit(solution)/shard_map/reshape | solution.py:200
  60.3 1.1 %collective-permute-start.2 = (bf16[48,2176]{1,0:T(8,128)(2,1)S(1)}, bf16[48,2176]{1,0:T(8,128)(2,1)S(1)}, u32[]{:S(2)}, u32[]{:S(2)}) collective-permute-start(bf16[48,2176]{1,0:T(8,128)(2,1)S(1)} %get-tuple-element.22), channel_id=1, source_target_pairs={{0,4},{4,8},{8,12},{12,16},{16,20},{20,24},{24,28},{28,0},{1,5},{5... | collective-permute-start | bytes 626696 | tf_op jit(solution)/shard_map/ppermute | solution.py:61
  61.5 3.7 %collective-permute-start.6 = (bf16[48,2176]{1,0:T(8,128)(2,1)S(1)}, bf16[48,2176]{1,0:T(8,128)(2,1)S(1)}, u32[]{:S(2)}, u32[]{:S(2)}) collective-permute-start(bf16[48,2176]{1,0:T(8,128)(2,1)S(1)} %get-tuple-element.25), channel_id=1, source_target_pairs={{0,28},{4,0},{8,4},{12,8},{16,12},{20,16},{24,20},{28,24},{1,29},{... | collective-permute-start | bytes 626696 | tf_op jit(solution)/shard_map/ppermute | solution.py:61
  65.1 3.8 %bitcast_reduce_fusion = (f32[96,2,2,8]{3,1,2,0:T(2,128)S(1)}, f32[96,2,2,8,64]{4,3,2,1,0:T(8,128)S(1)}) fusion(bf16[96,64,2,128,1]{3,2,1,0,4:T(2,128)(2,1)} %bitcast.104, bf16[96,2,2,8,128]{4,3,2,1,0:T(8,128)(2,1)S(1)} %reshape.177, pred[96,64]{1,0:T(8,128)(4,1)S(1)} %iota_compare_fusion.4), kind=kOutput, calls=%fused_computation.15 | convolution fusion | flops 50918400 | bytes 4737024 | tf_op jit(solution)/shard_map/rthgd,rjhd->rthgj/dot_general | solution.py:204
  69.0 2.2 %fusion.12 = f32[96,2,2,8,128]{4,3,1,2,0:T(8,128)} fusion(bf16[96,64,2,128,1]{3,2,1,0,4:T(2,128)(2,1)S(1)} %bitcast.110, f32[96,2,2,8,64]{4,3,2,1,0:T(8,128)S(1)} %get-tuple-element.73, f32[96,2,2,8]{3,1,2,0:T(2,128)S(1)} %get-tuple-element.72), kind=kOutput, calls=%fused_computation.19 | convolution fusion | flops 50724864 | bytes 5517312 | tf_op jit(solution)/shard_map/rthgj,rjhd->rthgd/dot_general | solution.py:212
  71.1 1.8 %fusion.16 = f32[96,2,2,8]{3,1,2,0:T(2,128)} fusion(f32[96,2,2,8,64]{4,3,2,1,0:T(8,128)S(1)} %get-tuple-element.73, f32[96,2,2,8]{3,1,2,0:T(2,128)S(1)} %get-tuple-element.72), kind=kLoop, calls=%fused_computation.21 | loop fusion | flops 390144 | bytes 811008 | tf_op jit(solution)/shard_map/reduce_sum | solution.py:211
  73.0 19.8 %shard_map.121 = f32[192,512]{1,0:T(8,128)S(1)} custom-call(bf16[48,2176]{1,0:T(8,128)(2,1)S(1)} %get-tuple-element.58.refs_0_, bf16[48,2176]{1,0:T(8,128)(2,1)S(1)} %collective-permute-done.2.refs_1_, bf16[48,2176]{1,0:T(8,128)(2,1)S(1)} %collective-permute-done.3.refs_2_, bf16[48,2176]{1,0:T(8,128)(2,1)S(1)} %collective-permute-done.refs_3_, ...), custom_call_target="tpu_custom_call" | custom-call | tf_op jit(solution)/shard_map/pallas_call | solution.py:172
  93.0 0.3 copy.86
  93.5 0.7 slice_bitcast_fusion.5
  94.2 1.3 %multiply_subtract_fusion = (bf16[96,2,2,64]{3,1,2,0:T(2,128)(2,1)S(1)}, bf16[96,2,2,64]{3,1,2,0:T(2,128)(2,1)S(1)}) fusion(f32[96,2,2,128]{3,1,2,0:T(2,128)S(1)} %slice_bitcast_fusion, f32[96,2,64]{2,1,0:T(2,128)} %get-tuple-element.70, f32[96,2,64]{2,1,0:T(2,128)} %get-tuple-element.69), kind=kLoop, calls=%fused_computation.50 | loop fusion | flops 196608 | bytes 393216 | tf_op jit(solution)/shard_map/sub | solution.py:27
  95.5 0.9 fusion.49
  96.4 3.7 %fusion.46 = (f32[96,2,2,8]{3,1,2,0:T(2,128)S(1)}, f32[96,2,2,8,2]{3,4,1,2,0:T(2,128)S(1)}) fusion(bf16[96,2,2,8,128]{4,3,2,1,0:T(8,128)(2,1)S(1)} %reshape.177, pred[2,2]{1,0:T(4,128)(4,1)S(1)} %iota_compare_fusion.6, bf16[96,2,2,64]{3,1,2,0:T(2,128)(2,1)S(1)} %get-tuple-element.64, bf16[96,2,2,64]{3,1,2,0:T(2,128)(2,1)S(1)} %get-tuple-element.63), kind=kOutput, calls=%fused_computation.90 | convolution fusion | flops 1784832 | bytes 921604 | tf_op jit(solution)/shard_map/rthgd,rshd->rthgs/dot_general | solution.py:227
  100.3 0.8 fusion.31
  101.3 0.5 fusion.30
  102.3 1.5 %add_convert_fusion = bf16[96,2,2,8,128]{4,3,1,2,0:T(8,128)(2,1)S(1)} fusion(f32[96,2,2,8,128]{4,3,1,2,0:T(8,128)S(1)} %copy-done.8, f32[96,2,128]{2,1,0:T(2,128)S(1)} %get-tuple-element.68, f32[96,2,2,8]{3,1,2,0:T(2,128)S(1)} %bitcast.115, f32[96,2,128]{2,1,0:T(2,128)S(1)} %get-tuple-element.67, f32[96,2,2,8]{3,1,2,0:T(2,128)S(1)} %bitcast.114, ...), kind=kLoop, calls=%fused_computation.17 | loop fusion | flops 2359296 | bytes 2592768 | tf_op jit(solution)/shard_map/convert_element_type | solution.py:241
  104.0 1.1 %reshape.186 = bf16[96,2,2048]{2,1,0:T(2,128)(2,1)} reshape(bf16[96,2,2,8,128]{4,3,2,1,0:T(8,128)(2,1)S(1)} %copy.54) | data formatting | bytes 1572864
  (59 shorter events, 2.5 us)
Async XLA Ops:
  0.6 6.6 %copy-start.2 = (bf16[96,2,8192]{2,1,0:T(2,128)(2,1)S(1)}, bf16[96,2,8192]{2,1,0:T(2,128)(2,1)}, u32[]{:S(2)}) copy-start(bf16[96,2,8192]{2,1,0:T(2,128)(2,1)} %param.10) | copy-start | bytes 9437188
  0.6 6.2 %copy-start.12 = (s32[96]{0:T(128)S(1)}, s32[96]{0:T(128)}, u32[]{:S(2)}) copy-start(s32[96]{0:T(128)} %param.15) | copy-start | bytes 1156
  7.2 17.3 %copy-start.1 = (bf16[8192,2,256]{2,1,0:T(2,128)(2,1)S(1)}, bf16[8192,2,256]{2,1,0:T(2,128)(2,1)}, u32[]{:S(2)}) copy-start(bf16[8192,2,256]{2,1,0:T(2,128)(2,1)} %param.12) | copy-start | bytes 25165828
  10.1 1.7 %copy-start.3 = (bf16[2,96,8192]{2,1,0:T(8,128)(2,1)}, bf16[2,96,8192]{2,1,0:T(8,128)(2,1)S(1)}, u32[]{:S(2)}) copy-start(bf16[2,96,8192]{2,1,0:T(8,128)(2,1)S(1)} %fusion.2) | copy-start | bytes 9437188
  13.6 44.2 %collective-permute-start = (bf16[48,2176]{1,0:T(8,128)(2,1)}, bf16[48,2176]{1,0:T(8,128)(2,1)S(1)}, u32[]{:S(2)}, u32[]{:S(2)}) collective-permute-start(bf16[48,2176]{1,0:T(8,128)(2,1)} %get-tuple-element.55), channel_id=1, source_target_pairs={{0,12},{4,16},{8,20},{12,24},{16,28},{20,0},{24,4},{28,8},{1,13},{... | collective-permute-start | bytes 626696 | tf_op jit(solution)/shard_map/ppermute | solution.py:61
  17.6 40.3 %collective-permute-start.1 = (bf16[48,2176]{1,0:T(8,128)(2,1)S(1)}, bf16[48,2176]{1,0:T(8,128)(2,1)S(1)}, u32[]{:S(2)}, u32[]{:S(2)}) collective-permute-start(bf16[48,2176]{1,0:T(8,128)(2,1)S(1)} %get-tuple-element.54), channel_id=1, source_target_pairs={{0,16},{4,20},{8,24},{12,28},{16,0},{20,4},{24,8},{28,12},{1,17},{... | collective-permute-start | bytes 626696 | tf_op jit(solution)/shard_map/ppermute | solution.py:61
  20.2 52.7 %collective-permute-start.3 = (bf16[48,2176]{1,0:T(8,128)(2,1)}, bf16[48,2176]{1,0:T(8,128)(2,1)S(1)}, u32[]{:S(2)}, u32[]{:S(2)}) collective-permute-start(bf16[48,2176]{1,0:T(8,128)(2,1)} %get-tuple-element.53), channel_id=1, source_target_pairs={{0,8},{4,12},{8,16},{12,20},{16,24},{20,28},{24,0},{28,4},{1,9},{5... | collective-permute-start | bytes 626696 | tf_op jit(solution)/shard_map/ppermute | solution.py:61
  20.4 52.5 %collective-permute-start.4 = (bf16[48,2176]{1,0:T(8,128)(2,1)}, bf16[48,2176]{1,0:T(8,128)(2,1)S(1)}, u32[]{:S(2)}, u32[]{:S(2)}) collective-permute-start(bf16[48,2176]{1,0:T(8,128)(2,1)} %get-tuple-element.52), channel_id=1, source_target_pairs={{0,20},{4,24},{8,28},{12,0},{16,4},{20,8},{24,12},{28,16},{1,21},{... | collective-permute-start | bytes 626696 | tf_op jit(solution)/shard_map/ppermute | solution.py:61
  23.1 49.9 %collective-permute-start.5 = (bf16[48,2176]{1,0:T(8,128)(2,1)}, bf16[48,2176]{1,0:T(8,128)(2,1)S(1)}, u32[]{:S(2)}, u32[]{:S(2)}) collective-permute-start(bf16[48,2176]{1,0:T(8,128)(2,1)} %get-tuple-element.51), channel_id=1, source_target_pairs={{0,24},{4,28},{8,0},{12,4},{16,8},{20,12},{24,16},{28,20},{1,25},{... | collective-permute-start | bytes 626696 | tf_op jit(solution)/shard_map/ppermute | solution.py:61
  37.5 5.5 %copy-start.4 = (bf16[2,96,8192]{2,1,0:T(8,128)(2,1)S(1)}, bf16[2,96,8192]{2,1,0:T(8,128)(2,1)}, u32[]{:S(2)}) copy-start(bf16[2,96,8192]{2,1,0:T(8,128)(2,1)} %copy-done.3) | copy-start | bytes 9437188
  49.6 5.6 %copy-start.10 = (bf16[4,2,64,256]{3,2,1,0:T(8,128)(2,1)S(1)}, bf16[4,2,64,256]{3,2,1,0:T(8,128)(2,1)}, u32[]{:S(2)}) copy-start(bf16[4,2,64,256]{3,2,1,0:T(8,128)(2,1)} %param.14) | copy-start | bytes 786436
  49.7 5.6 %copy-start.11 = (s32[96]{0:T(128)S(1)}, s32[96]{0:T(128)}, u32[]{:S(2)}) copy-start(s32[96]{0:T(128)} %param.19) | copy-start | bytes 1156
  60.3 8.6 %copy-start.7 = (bf16[96,64,2,128]{3,2,1,0:T(2,128)(2,1)S(1)}, bf16[96,64,2,128]{3,2,1,0:T(2,128)(2,1)}, u32[]{:S(2)}) copy-start(bf16[96,64,2,128]{3,2,1,0:T(2,128)(2,1)} %reshape.179) | copy-start | bytes 9437188
  60.3 12.6 %collective-permute-start.2 = (bf16[48,2176]{1,0:T(8,128)(2,1)S(1)}, bf16[48,2176]{1,0:T(8,128)(2,1)S(1)}, u32[]{:S(2)}, u32[]{:S(2)}) collective-permute-start(bf16[48,2176]{1,0:T(8,128)(2,1)S(1)} %get-tuple-element.22), channel_id=1, source_target_pairs={{0,4},{4,8},{8,12},{12,16},{16,20},{20,24},{24,28},{28,0},{1,5},{5... | collective-permute-start | bytes 626696 | tf_op jit(solution)/shard_map/ppermute | solution.py:61
  61.5 11.5 %collective-permute-start.6 = (bf16[48,2176]{1,0:T(8,128)(2,1)S(1)}, bf16[48,2176]{1,0:T(8,128)(2,1)S(1)}, u32[]{:S(2)}, u32[]{:S(2)}) collective-permute-start(bf16[48,2176]{1,0:T(8,128)(2,1)S(1)} %get-tuple-element.25), channel_id=1, source_target_pairs={{0,28},{4,0},{8,4},{12,8},{16,12},{20,16},{24,20},{28,24},{1,29},{... | collective-permute-start | bytes 626696 | tf_op jit(solution)/shard_map/ppermute | solution.py:61
  69.0 2.2 %copy-start.5 = (f32[96,2,2,8]{3,1,2,0:T(2,128)}, f32[96,2,2,8]{3,1,2,0:T(2,128)S(1)}, u32[]{:S(2)}) copy-start(f32[96,2,2,8]{3,1,2,0:T(2,128)S(1)} %get-tuple-element.72) | copy-start | bytes 36868
  69.0 4.0 %copy-start = (bf16[4,2048,128]{2,1,0:T(8,128)(2,1)S(1)}, bf16[4,2048,128]{2,1,0:T(8,128)(2,1)}, u32[]{:S(2)}) copy-start(bf16[4,2048,128]{2,1,0:T(8,128)(2,1)} %refs_8_.1) | copy-start | bytes 6291460
  92.8 7.4 %copy-start.6 = (f32[96,2,2,8]{3,1,2,0:T(2,128)S(1)}, f32[96,2,2,8]{3,1,2,0:T(2,128)}, u32[]{:S(2)}) copy-start(f32[96,2,2,8]{3,1,2,0:T(2,128)} %copy-done.5) | copy-start | bytes 36868
  93.3 7.7 %copy-start.9 = (f32[96,2,2,8]{3,1,2,0:T(2,128)S(1)}, f32[96,2,2,8]{3,1,2,0:T(2,128)}, u32[]{:S(2)}) copy-start(f32[96,2,2,8]{3,1,2,0:T(2,128)} %fusion.16) | copy-start | bytes 36868
  100.1 2.2 %copy-start.8 = (f32[96,2,2,8,128]{4,3,1,2,0:T(8,128)S(1)}, f32[96,2,2,8,128]{4,3,1,2,0:T(8,128)}, u32[]{:S(2)}) copy-start(f32[96,2,2,8,128]{4,3,1,2,0:T(8,128)} %fusion.12) | copy-start | bytes 4718596
